TPU v7x, 128 devices: a whole 4x4x4 slice. The times are simulated.
128 devices in a mesh: row: 8 (over y, core), col: 16 (over z, x).
Axes of the slice: x: 4, y: 4, z: 4, core: 2. Of those that a mesh axis runs over, the one named last changes fastest.
Arguments:
- user_factors: float32 [16384, 128], P('row'), may hold values from -6 to 6
- item_factors: float32 [131072, 128], P(('row', 'col')), may hold values from -0.015625 to 0.015625
- fetch_list: int32 [8, 16, 128, 1], P('row', 'col'), may hold values from 0 to 7
- tile_user: int32 [8, 16, 32], P('row', 'col'), may hold values from 0 to 15
- tile_slot: int32 [8, 16, 32], P('row', 'col'), may hold values from 0 to 127
- entry_row: int32 [8, 16, 32, 512], P('row', 'col'), may hold values from 0 to 127
- entry_col: int32 [8, 16, 32, 512], P('row', 'col'), may hold values from 0 to 127
- entry_count: int32 [8, 16, 32, 512], P('row', 'col'), may hold values from 1 to 8
- tile_count: int32 [8, 16], P('row', 'col'), may hold values from 4 to 32, as said below
Outputs:
- solved: float32 [16384, 128], P('row')
Inputs may be any that keep to these rules, and one draw needn't show every extreme that they name: `tile_count`: at least 4 tiles live on every device; some device has all 32 live in every draw.
All inputs are finite; a program needn't handle non-finite values.
Results may differ from a plain program's by a relative error of at most 0.0003.
Values sent between devices are 32-bit elements; how exact they have to be, the bound alone decides.
A program may use at most 128 MiB of HBM per device.

v0:
```python
import jax
import jax.numpy as jnp
from jax import lax
from jax.sharding import PartitionSpec as P

K = 128
BLOCK = 128
ITERS = 3
HIGHEST = lax.Precision.HIGHEST
CONFIDENCE_SCALE = 40.0
RIDGE = 0.5
EPSILON = 1e-06


def conjugate(iterate, residual, apply_full):
    direction = residual
    norm_now = jnp.sum(residual * residual, axis=1, keepdims=True)
    for iteration in range(ITERS):
        image = apply_full(direction)
        alpha = norm_now / (jnp.sum(direction * image, axis=1, keepdims=True) + EPSILON)
        iterate = iterate + alpha * direction
        residual = residual - alpha * image
        norm_next = jnp.sum(residual * residual, axis=1, keepdims=True)
        direction = residual + norm_next / (norm_now + EPSILON) * direction
        norm_now = norm_next
    return iterate


def shards(
    user_factors,
    item_factors,
    fetch_list,
    tile_user,
    tile_slot,
    entry_row,
    entry_col,
    entry_count,
    tile_count,
):
    user_rows = user_factors.shape[0]
    user_blocks = user_rows // BLOCK
    local_blocks = item_factors.reshape(-1, BLOCK, K)
    wanted = fetch_list[0, 0]
    peers = wanted.shape[0]
    width = wanted.shape[1]
    asked = lax.all_to_all(wanted, ("row", "col"), split_axis=0, concat_axis=0, tiled=True)
    served = jnp.take(local_blocks, asked.reshape(-1), axis=0).reshape(peers, width, BLOCK, K)
    fetched = lax.all_to_all(
        served, ("row", "col"), split_axis=0, concat_axis=0, tiled=True
    ).reshape(-1, BLOCK, K)
    gram = lax.psum(
        jnp.dot(
            item_factors.T, item_factors, precision=HIGHEST, preferred_element_type=jnp.float32
        ),
        ("row", "col"),
    )
    users = tile_user[0, 0]
    slot_ids = tile_slot[0, 0]
    tiles = users.shape[0]
    tile_index = jnp.arange(tiles, dtype=jnp.int32)
    alive = (tile_index < tile_count[0, 0]).astype(jnp.float32)
    excess = CONFIDENCE_SCALE * entry_count[0, 0].astype(jnp.float32)
    weight_fit = excess * alive[:, None]
    weight_rhs = (1.0 + excess) * alive[:, None]
    rows_in = entry_row[0, 0]
    cols_in = entry_col[0, 0]
    block_ids = jnp.arange(BLOCK, dtype=jnp.int32)
    row_onehot = (rows_in[:, :, None] == block_ids[None, None, :]).astype(jnp.float32)
    col_onehot = (cols_in[:, :, None] == block_ids[None, None, :]).astype(jnp.float32)
    dense_fit = jnp.einsum(
        "tnu,tni->tui", row_onehot * weight_fit[:, :, None], col_onehot, precision=HIGHEST
    )
    dense_rhs = jnp.einsum(
        "tnu,tni->tui", row_onehot * weight_rhs[:, :, None], col_onehot, precision=HIGHEST
    )
    item_tiles = jnp.take(fetched, slot_ids, axis=0)
    owner_onehot = (users[None, :] == jnp.arange(user_blocks, dtype=jnp.int32)[:, None]).astype(
        jnp.float32
    )

    def tile_terms(vector):
        picked_users = jnp.take(vector.reshape(user_blocks, BLOCK, K), users, axis=0)
        scores = jnp.einsum("tuk,tik->tui", picked_users, item_tiles, precision=HIGHEST)
        pulled = jnp.einsum("tui,tik->tuk", dense_fit * scores, item_tiles, precision=HIGHEST)
        return jnp.einsum("bt,tuk->buk", owner_onehot, pulled, precision=HIGHEST).reshape(
            user_rows, K
        )

    rhs_pulled = jnp.einsum("tui,tik->tuk", dense_rhs, item_tiles, precision=HIGHEST)
    rhs_local = jnp.einsum("bt,tuk->buk", owner_onehot, rhs_pulled, precision=HIGHEST).reshape(
        user_rows, K
    )

    def extra(vector):
        return (
            jnp.dot(vector, gram, precision=HIGHEST, preferred_element_type=jnp.float32)
            + RIDGE * vector
        )

    start_terms = rhs_local - tile_terms(user_factors)

    def apply_whole(vector):
        return lax.psum(tile_terms(vector), "col") + extra(vector)

    residual = lax.psum(start_terms, "col") - extra(user_factors)
    solved = conjugate(user_factors, residual, apply_whole)
    return solved


def solution(mesh):
    return jax.shard_map(
        shards,
        mesh=mesh,
        in_specs=(
            P("row", None),
            P(("row", "col"), None),
            P("row", "col", None, None),
            P("row", "col", None),
            P("row", "col", None),
            P("row", "col", None, None),
            P("row", "col", None, None),
            P("row", "col", None, None),
            P("row", "col"),
        ),
        out_specs=P("row", None),
        check_vma=False,
    )
```

profile of v0, /device:TPU:0, one launch (start us, length us, event | category | flops | bytes accessed | tf_op | source)
XLA Modules:
  0.0 695.5 jit_solution(1226374862709490610)
XLA Ops:
  7.4 20.4 %all_to_all.20 = s32[128,1,1]{2,1,0:T(1,128)S(1)} all-to-all(s32[128,1,1]{2,1,0:T(1,128)S(1)} %copy.50), channel_id=1, replica_groups=mesh['row'=8,'col'=16] {'row','col'}, dimensions={0} | all-to-all | bytes 1024 | tf_op jit(solution)/shard_map/all_to_all | solution.py:46
  30.2 4.3 gather_fusion
  34.5 7.2 %bitcast_select_fusion = f32[128,1,128,128]{3,2,1,0:T(8,128)} fusion(f32[128,128,128]{2,1,0:T(8,128)} %gather_fusion, pred[128]{0:T(512)(128)(4,1)S(1)} %compare_and_fusion.1), kind=kLoop, calls=%fused_computation.6 | loop fusion | flops 2097152 | bytes 16777344 | tf_op jit(solution)/shard_map/jit(_take)/select_n | solution.py:47
  41.7 6.1 all-to-all-start.1
  52.4 8.1 %fusion = f32[32,128,128]{2,1,0:T(8,128)} fusion(f32[32,512]{1,0:T(8,128)S(1)} %get-tuple-element.11, s32[32,512]{1,0:T(8,128)S(1)} %bitcast.99, s32[32,512]{1,0:T(8,128)S(1)} %bitcast.101), kind=kOutput, calls=%fused_computation.7 | convolution fusion | flops 3227516928 | bytes 2293760 | tf_op jit(solution)/shard_map/tnu,tni->tui/dot_general | solution.py:70
  60.5 8.2 %fusion.2 = f32[32,128,128]{2,1,0:T(8,128)} fusion(s32[32,512]{1,0:T(8,128)S(1)} %bitcast.100, f32[32,512]{1,0:T(8,128)S(1)} %get-tuple-element.10, s32[32,512]{1,0:T(8,128)S(1)} %bitcast.102), kind=kOutput, calls=%fused_computation.10 | convolution fusion | flops 3227516928 | bytes 2293760 | tf_op jit(solution)/shard_map/tnu,tni->tui/dot_general | solution.py:73
  68.8 79.1 %all-to-all-done.1 = f32[128,1,128,128]{3,2,1,0:T(8,128)} async-done(((f32[128,1,128,128]{3,2,1,0:T(8,128)}), f32[128,1,128,128]{3,2,1,0:T(8,128)}, u32[]{:S(2)}, u32[]{:S(2)}) %all-to-all-start.1) | async-done | bytes 8388640 | tf_op jit(solution)/shard_map/all_to_all | solution.py:48
  147.9 4.1 gather_fusion.1
  152.0 3.9 fusion.50
  155.9 4.6 fusion.28
  168.4 2.6 copy.54
  172.3 81.8 %all-reduce.8.cloned.1.call-done = f32[128,128]{1,0:T(8,128)} async-done(((f32[128,128]{1,0:T(8,128)}), f32[128,128]{1,0:T(8,128)}) %all-reduce.8.cloned.1.call-update) | async-done | bytes 65552 | tf_op jit(solution)/shard_map/psum | solution.py:51
  254.1 90.1 %all-reduce.6.cloned.1.call-done = f32[2048,128]{0,1:T(8,128)} async-done(((f32[2048,128]{0,1:T(8,128)}), f32[2048,128]{0,1:T(8,128)}) %all-reduce.6.cloned.1.call-update) | async-done | bytes 1048592 | tf_op jit(solution)/shard_map/psum | solution.py:105
  344.2 3.0 fusion.13
  348.5 3.2 gather_fusion.3
  351.7 6.3 fusion.26
  358.0 3.6 fusion.34
  361.7 3.1 copy.69
  369.0 86.0 %all-reduce.10.cloned.1.call-done = f32[2048,128]{0,1:T(8,128)} async-done(((f32[2048,128]{0,1:T(8,128)}), f32[2048,128]{0,1:T(8,128)}) %all-reduce.10.cloned.1.call-update) | async-done | bytes 1048592 | tf_op jit(solution)/shard_map/psum | solution.py:103
  459.9 2.6 copy.79
  462.4 3.2 gather_fusion.4
  465.6 6.3 fusion.24
  472.0 3.6 fusion.32
  475.6 3.1 copy.72
  482.7 86.2 %all-reduce.12.cloned.1.call-done = f32[2048,128]{0,1:T(8,128)} async-done(((f32[2048,128]{0,1:T(8,128)}), f32[2048,128]{0,1:T(8,128)}) %all-reduce.12.cloned.1.call-update) | async-done | bytes 1048592 | tf_op jit(solution)/shard_map/psum | solution.py:103
  568.8 3.2 multiply_reduce_fusion.1
  576.1 3.2 gather_fusion.5
  579.3 6.3 fusion.22
  585.6 3.6 fusion.30
  593.8 86.4 %all-reduce.14.cloned.1.call-done = f32[2048,128]{0,1:T(8,128)} async-done(((f32[2048,128]{0,1:T(8,128)}), f32[2048,128]{0,1:T(8,128)}) %all-reduce.14.cloned.1.call-update) | async-done | bytes 1048592 | tf_op jit(solution)/shard_map/psum | solution.py:103
  680.2 3.0 fusion.41
  683.3 3.0 multiply_add_fusion
  (86 shorter events, 41.7 us)
Async XLA Ops:
  6.5 23.6 %copy-start = (f32[1024,128]{1,0:T(8,128)S(1)}, f32[1024,128]{1,0:T(8,128)}, u32[]{:S(2)}) copy-start(f32[1024,128]{1,0:T(8,128)} %param.12) | copy-start | bytes 1572868
  41.7 8.5 %copy-start.14 = (s32[1,1,32]{2,1,0:T(1,128)S(1)}, s32[1,1,32]{2,1,0:T(1,128)}, u32[]{:S(2)}) copy-start(s32[1,1,32]{2,1,0:T(1,128)} %param.14) | copy-start | bytes 388
  41.7 106.2 %all-to-all-start.1 = ((f32[128,1,128,128]{3,2,1,0:T(8,128)}), f32[128,1,128,128]{3,2,1,0:T(8,128)}, u32[]{:S(2)}, u32[]{:S(2)}) async-start(f32[128,1,128,128]{3,2,1,0:T(8,128)} %bitcast_select_fusion), calls=%async_computation.1 | async-start | bytes 16777216 | tf_op jit(solution)/shard_map/all_to_all | solution.py:48
  47.8 2.5 copy-start.10
  47.8 206.3 %all-reduce.8.cloned.1.call-start = ((), (), s32[]{:S(2)}) async-start(), calls=%async_computation.3 | async-start | bytes 131072 | tf_op jit(solution)/shard_map/psum | solution.py:51
  49.5 294.7 %all-reduce.6.cloned.1.call-start = ((), (), s32[]{:S(2)}) async-start(), calls=%async_computation.2 | async-start | bytes 2097152 | tf_op jit(solution)/shard_map/psum | solution.py:105
  50.2 2.0 copy-start.15
  50.3 2.1 copy-start.13
  50.3 2.2 copy-start.16
  50.3 2.2 copy-start.17
  151.9 4.0 copy-start.11
  155.9 4.6 copy-start.2
  171.0 284.0 %all-reduce.10.cloned.1.call-start = ((), (), s32[]{:S(2)}) async-start(), calls=%async_computation.4 | async-start | bytes 2097152 | tf_op jit(solution)/shard_map/psum | solution.py:103
  351.7 6.3 copy-start.3
  367.2 87.8 %copy-start.12 = (f32[128,128]{1,0:T(8,128)S(1)}, f32[128,128]{1,0:T(8,128)}, u32[]{:S(2)}) copy-start(f32[128,128]{1,0:T(8,128)} %all-reduce.8.cloned.1.call-done) | copy-start | bytes 196612
  368.5 200.3 %all-reduce.12.cloned.1.call-start = ((), (), s32[]{:S(2)}) async-start(), calls=%async_computation.5 | async-start | bytes 2097152 | tf_op jit(solution)/shard_map/psum | solution.py:103
  457.7 1.0 copy-start.8
  465.6 6.3 copy-start.4
  482.4 197.8 %all-reduce.14.cloned.1.call-start = ((), (), s32[]{:S(2)}) async-start(), calls=%async_computation.6 | async-start | bytes 2097152 | tf_op jit(solution)/shard_map/psum | solution.py:103
  568.8 3.3 copy-start.9
  568.8 3.5 copy-start.6
  579.3 6.3 copy-start.5
  593.8 89.5 %copy-start.7 = (f32[2048,128]{0,1:T(8,128)S(1)}, f32[2048,128]{0,1:T(8,128)}, u32[]{:S(2)}) copy-start(f32[2048,128]{0,1:T(8,128)} %multiply_add_fusion.2) | copy-start | bytes 3145732
  683.3 5.5 copy-start.1
Sparse Core Ops, SparseCore 0:
  53.4 200.6 all-reduce.7
  257.7 86.4 all-reduce.5
  368.7 86.2 all-reduce.9
  482.6 86.2 all-reduce.11
  593.9 86.2 all-reduce.13
where the time goes:
time: 702 us; the launch traced here: 696 us
  waiting for transfers between devices  510 us (73%)
  matrix products  80.1 us (11%)
  local copies, waits for them, and re-layouts  48.6 us (7%)
  blocking collectives  20.4 us (3%)
  other arithmetic  15.5 us (2%)
  between operations  14.4 us (2%)
    psum x3, waiting for transfers between devices, apply_whole(): return lax.psum(tile_terms(vector), 'col') + extra(vector)  259 us
    psum x1, waiting for transfers between devices, shards(): residual = lax.psum(start_terms, 'col') - extra(user_factors)  90.1 us
    psum x1, waiting for transfers between devices, shards(): lax.psum(jnp.dot(item_factors.T, item_factors, precision=HIGHEST, preferr...  81.8 us
    all_to_all x1, waiting for transfers between devices, shards(): lax.all_to_all(served, ('row', 'col'), split_axis=0, concat_axis=0, tiled...  79.1 us
    dot_general x4, matrix products, tile_terms(): jnp.einsum('tuk,tik->tui', picked_users, item_tiles, precision=HIGHEST)  23.5 us
    all_to_all x1, blocking collectives, shards(): lax.all_to_all(wanted, ('row', 'col'), split_axis=0, concat_axis=0, tiled...  20.4 us
  transfers between devices with their start and end apart: 6, of which 6 were waited for; matrix products, arithmetic and copies ran while one was open for 6% of the time, Pallas kernels for 0%

commit v1 on v0

--- a/solution.py
+++ b/solution.py
@@ -102,7 +102,7 @@
     def apply_whole(vector):
         return lax.psum(tile_terms(vector), "col") + extra(vector)
 
-    residual = lax.psum(start_terms, "col") - extra(user_factors)
+    residual = jnp.sum(lax.all_gather(start_terms, "col"), axis=0) - extra(user_factors)
     solved = conjugate(user_factors, residual, apply_whole)
     return solved
 

time: 702 us -> 747 us (1.064)
  waiting for transfers between devices: 510 us -> 538 us
  other arithmetic: 15.5 us -> 27.4 us
    all_gather x0 -> x1, waiting for transfers between devices: none -> 117 us  [shards(): lax.all_gather(start_terms, 'col')]
    psum x1 -> x0, waiting for transfers between devices: 90.1 us -> none  [shards(): residual = lax.psum(start_terms, 'col') - extra(user_factors)]
    reduce_sum x0 -> x1, other arithmetic: none -> 7.65 us  [shards(): jnp.sum(lax.all_gather(start_terms, 'col'), axis=0) - extra(user_factors)]
  transfers between devices with their start and end apart: 6 -> 6, of which waited for: 6 -> 6; matrix products, arithmetic and copies ran while one was open for 6% -> 4% of each run, Pallas kernels for 0% -> 0%
where the time goes in v1:
time: 747 us; the launch traced here: 741 us
  waiting for transfers between devices  538 us (72%)
  matrix products  81.6 us (11%)
  local copies, waits for them, and re-layouts  51.4 us (7%)
  other arithmetic  27.4 us (4%)
  blocking collectives  20.4 us (3%)
  between operations  15.8 us (2%)
    psum x3, waiting for transfers between devices, apply_whole(): return lax.psum(tile_terms(vector), 'col') + extra(vector)  259 us
    all_gather x1, waiting for transfers between devices, shards(): lax.all_gather(start_terms, 'col')  117 us
    all_to_all x1, waiting for transfers between devices, shards(): lax.all_to_all(served, ('row', 'col'), split_axis=0, concat_axis=0, tiled...  81 us
    psum x1, waiting for transfers between devices, shards(): lax.psum(jnp.dot(item_factors.T, item_factors, precision=HIGHEST, preferr...  80.5 us
    dot_general x4, matrix products, tile_terms(): jnp.einsum('tuk,tik->tui', picked_users, item_tiles, precision=HIGHEST)  23.5 us
    all_to_all x1, blocking collectives, shards(): lax.all_to_all(wanted, ('row', 'col'), split_axis=0, concat_axis=0, tiled...  20.4 us
  transfers between devices with their start and end apart: 6, of which 6 were waited for; matrix products, arithmetic and copies ran while one was open for 4% of the time, Pallas kernels for 0%

profile of v1, /device:TPU:0, one launch (start us, length us, event | category | flops | bytes accessed | tf_op | source)
XLA Modules:
  0.0 740.8 jit_solution(10976611587351090543)
XLA Ops:
  8.2 20.4 %all_to_all.20 = s32[128,1,1]{2,1,0:T(1,128)S(1)} all-to-all(s32[128,1,1]{2,1,0:T(1,128)S(1)} %copy.49), channel_id=1, replica_groups=mesh['row'=8,'col'=16] {'row','col'}, dimensions={0} | all-to-all | bytes 1024 | tf_op jit(solution)/shard_map/all_to_all | solution.py:46
  31.0 4.3 gather_fusion
  35.3 7.2 bitcast_select_fusion
  42.5 6.1 all-to-all-start.1
  51.6 8.1 %fusion = f32[32,128,128]{2,1,0:T(8,128)} fusion(f32[32,512]{1,0:T(8,128)S(1)} %get-tuple-element.11, s32[32,512]{1,0:T(8,128)S(1)} %bitcast.99, s32[32,512]{1,0:T(8,128)S(1)} %bitcast.101), kind=kOutput, calls=%fused_computation.7 | convolution fusion | flops 3227516928 | bytes 2293760 | tf_op jit(solution)/shard_map/tnu,tni->tui/dot_general | solution.py:70
  59.6 8.2 %fusion.2 = f32[32,128,128]{2,1,0:T(8,128)} fusion(s32[32,512]{1,0:T(8,128)S(1)} %bitcast.100, f32[32,512]{1,0:T(8,128)S(1)} %get-tuple-element.10, s32[32,512]{1,0:T(8,128)S(1)} %bitcast.102), kind=kOutput, calls=%fused_computation.10 | convolution fusion | flops 3227516928 | bytes 2293760 | tf_op jit(solution)/shard_map/tnu,tni->tui/dot_general | solution.py:73
  67.9 81.0 %all-to-all-done.1 = f32[128,1,128,128]{3,2,1,0:T(8,128)} async-done(((f32[128,1,128,128]{3,2,1,0:T(8,128)}), f32[128,1,128,128]{3,2,1,0:T(8,128)}, u32[]{:S(2)}, u32[]{:S(2)}) %all-to-all-start.1) | async-done | bytes 8388640 | tf_op jit(solution)/shard_map/all_to_all | solution.py:48
  148.8 4.1 gather_fusion.1
  152.9 3.9 fusion.50
  156.9 4.6 fusion.28
  173.7 116.8 %all-gather.2.cloned.1.call-done = f32[16,2048,128]{2,1,0:T(8,128)} async-done(((f32[1,2048,128]{2,1,0:T(8,128)}), f32[16,2048,128]{2,1,0:T(8,128)}) %all-gather.2.cloned.1.call-update) | async-done | bytes 16777232 | tf_op jit(solution)/shard_map/all_gather | solution.py:105
  290.5 7.6 %reduce_sum.63 = f32[2048,128]{1,0:T(8,128)} reduce(f32[16,2048,128]{2,1,0:T(8,128)} %all-gather.2.cloned.1.call-done, f32[]{:T(128)} %constant.33.clone.1), dimensions={0}, to_apply=%region_0.0 | reduce | flops 3932160 | bytes 17825796 | tf_op jit(solution)/shard_map/reduce_sum | solution.py:105
  300.7 80.5 %all-reduce.5.cloned.1.call-done = f32[128,128]{1,0:T(8,128)} async-done(((f32[128,128]{1,0:T(8,128)}), f32[128,128]{1,0:T(8,128)}) %all-reduce.5.cloned.1.call-update) | async-done | bytes 65552 | tf_op jit(solution)/shard_map/psum | solution.py:51
  381.2 4.0 fusion.13
  387.7 3.2 gather_fusion.3
  391.0 6.3 fusion.26
  397.3 3.6 fusion.34
  400.9 3.5 copy.68
  408.2 86.7 %all-reduce.7.cloned.1.call-done = f32[2048,128]{0,1:T(8,128)} async-done(((f32[2048,128]{0,1:T(8,128)}), f32[2048,128]{0,1:T(8,128)}) %all-reduce.7.cloned.1.call-update) | async-done | bytes 1048592 | tf_op jit(solution)/shard_map/psum | solution.py:103
  495.0 3.1 multiply_reduce_fusion.3
  504.4 3.2 gather_fusion.4
  507.6 6.3 fusion.24
  513.9 3.6 fusion.32
  517.5 3.1 copy.71
  524.6 86.2 %all-reduce.9.cloned.1.call-done = f32[2048,128]{0,1:T(8,128)} async-done(((f32[2048,128]{0,1:T(8,128)}), f32[2048,128]{0,1:T(8,128)}) %all-reduce.9.cloned.1.call-update) | async-done | bytes 1048592 | tf_op jit(solution)/shard_map/psum | solution.py:103
  610.8 3.1 multiply_reduce_fusion.1
  620.7 3.2 gather_fusion.5
  624.0 6.3 fusion.22
  630.3 3.6 fusion.30
  638.4 86.4 %all-reduce.11.cloned.1.call-done = f32[2048,128]{0,1:T(8,128)} async-done(((f32[2048,128]{0,1:T(8,128)}), f32[2048,128]{0,1:T(8,128)}) %all-reduce.11.cloned.1.call-update) | async-done | bytes 1048592 | tf_op jit(solution)/shard_map/psum | solution.py:103
  724.8 3.0 fusion.41
  727.9 3.0 multiply_add_fusion
  (87 shorter events, 50.5 us)
Async XLA Ops:
  7.4 23.6 %copy-start = (f32[1024,128]{1,0:T(8,128)S(1)}, f32[1024,128]{1,0:T(8,128)}, u32[]{:S(2)}) copy-start(f32[1024,128]{1,0:T(8,128)} %param.12) | copy-start | bytes 1572868
  42.5 6.8 copy-start.14
  42.5 6.8 copy-start.10
  42.5 106.3 %all-to-all-start.1 = ((f32[128,1,128,128]{3,2,1,0:T(8,128)}), f32[128,1,128,128]{3,2,1,0:T(8,128)}, u32[]{:S(2)}, u32[]{:S(2)}) async-start(f32[128,1,128,128]{3,2,1,0:T(8,128)} %bitcast_select_fusion), calls=%async_computation.1 | async-start | bytes 16777216 | tf_op jit(solution)/shard_map/all_to_all | solution.py:48
  48.6 241.9 %all-gather.2.cloned.1.call-start = ((), (), s32[]{:S(2)}) async-start(), calls=%async_computation.2 | async-start | bytes 17825792 | tf_op jit(solution)/shard_map/all_gather | solution.py:105
  49.4 2.0 copy-start.15
  49.4 2.1 copy-start.13
  49.4 2.2 copy-start.16
  49.4 2.2 copy-start.17
  152.9 4.0 copy-start.11
  156.9 4.6 copy-start.4
  169.4 211.9 %all-reduce.5.cloned.1.call-start = ((), (), s32[]{:S(2)}) async-start(), calls=%async_computation.3 | async-start | bytes 131072 | tf_op jit(solution)/shard_map/psum | solution.py:51
  171.1 323.9 %all-reduce.7.cloned.1.call-start = ((), (), s32[]{:S(2)}) async-start(), calls=%async_computation.4 | async-start | bytes 2097152 | tf_op jit(solution)/shard_map/psum | solution.py:103
  391.0 6.3 copy-start.5
  406.8 88.2 %copy-start.12 = (f32[128,128]{1,0:T(8,128)S(1)}, f32[128,128]{1,0:T(8,128)}, u32[]{:S(2)}) copy-start(f32[128,128]{1,0:T(8,128)} %all-reduce.5.cloned.1.call-done) | copy-start | bytes 196612
  408.2 202.7 %all-reduce.9.cloned.1.call-start = ((), (), s32[]{:S(2)}) async-start(), calls=%async_computation.5 | async-start | bytes 2097152 | tf_op jit(solution)/shard_map/psum | solution.py:103
  498.1 2.6 copy-start.2
  499.7 1.0 copy-start.9
  507.6 6.3 copy-start.6
  524.4 200.4 %all-reduce.11.cloned.1.call-start = ((), (), s32[]{:S(2)}) async-start(), calls=%async_computation.6 | async-start | bytes 2097152 | tf_op jit(solution)/shard_map/psum | solution.py:103
  624.0 6.3 copy-start.7
  638.4 89.5 %copy-start.3 = (f32[2048,128]{0,1:T(8,128)S(1)}, f32[2048,128]{0,1:T(8,128)}, u32[]{:S(2)}) copy-start(f32[2048,128]{0,1:T(8,128)} %fusion.13) | copy-start | bytes 3145732
  638.4 89.5 %copy-start.8 = (f32[2048,128]{0,1:T(8,128)S(1)}, f32[2048,128]{0,1:T(8,128)}, u32[]{:S(2)}) copy-start(f32[2048,128]{0,1:T(8,128)} %multiply_add_fusion.2) | copy-start | bytes 3145732
  727.9 5.6 copy-start.1
Sparse Core Ops, SparseCore 0:
  169.5 120.9 all-gather.1
  408.3 86.6 all-reduce.6
  524.5 86.2 all-reduce.8
  638.6 86.2 all-reduce.10
Sparse Core Ops, SparseCore 1:
  174.6 206.6 all-reduce.4
